TPU v7x, 32 devices: a whole 2x2x4 slice. The times are simulated.
32 devices in a mesh: dp: 2 (over x), expert: 16 (over z, y, core).
Axes of the slice: x: 2, y: 2, z: 4, core: 2. Of those that a mesh axis runs over, the one named last changes fastest.
Arguments:
- tokens: bfloat16 [4096, 2048], P(('dp', 'expert')), may hold values from -6 to 6
- cotangent: bfloat16 [4096, 2048], P(('dp', 'expert')), may hold values from -0.875 to 0.875
- expert_ids: int32 [4096, 8], P(('dp', 'expert')), may hold values from 0 to 15, all different within a row; in each aligned block of 128 rows (0 to 127, 128 to 255, ...) at most 72 rows name the same one
- combine: float32 [4096, 8], P(('dp', 'expert')), may hold values from 0.02 to 0.5
- w_gate: bfloat16 [16, 2048, 512], P('expert'), may hold values from -0.125 to 0.125
- w_up: bfloat16 [16, 2048, 512], P('expert'), may hold values from -0.125 to 0.125
- w_down: bfloat16 [16, 512, 2048], P('expert'), may hold values from -0.25 to 0.25
- tangent_gate: bfloat16 [16, 2048, 512], P('expert'), may hold values from -0.125 to 0.125
Outputs:
- hvp_gate: float32 [16, 2048, 512], P('expert', 'dp')
- output_tangent: bfloat16 [4096, 2048], P(('dp', 'expert'))
Inputs may be any that keep to these rules, and one draw needn't show every extreme that they name: `expert_ids`: A row names 8 different experts; among the 128 rows of one device no expert is named by more than 72 rows, and in every draw some expert is named by exactly 72 rows of some device.
All inputs are finite; a program needn't handle non-finite values.
Results may differ from a plain program's by a relative error of at most 0.0057.
Values may be sent and summed in bfloat16 or wider, within the bound.
A program may use at most 128 MiB of HBM per device.

v0:
```python
import jax
import jax.numpy as jnp
from jax import lax
from jax.sharding import PartitionSpec as P


def silu_derivs(gate_act):
    squash = jax.nn.sigmoid(gate_act)
    first = squash * (1.0 + gate_act * (1.0 - squash))
    second = squash * (1.0 - squash) * (2.0 + gate_act * (1.0 - 2.0 * squash))
    return (first, second)


def forward_part(rows_flat, gate_e, up_e, down_e, tangent_e):
    gate_act = jnp.dot(rows_flat, gate_e, preferred_element_type=jnp.float32)
    up_act = jnp.dot(rows_flat, up_e, preferred_element_type=jnp.float32)
    gate_dot = jnp.dot(rows_flat, tangent_e, preferred_element_type=jnp.float32)
    first, second = silu_derivs(gate_act)
    lifted = (first * gate_dot * up_act).astype(jnp.bfloat16)
    term = jnp.dot(lifted, down_e, preferred_element_type=jnp.float32).astype(jnp.bfloat16)
    return (term, up_act * second * gate_dot)


def backward_part(scaled_flat, down_e, factor):
    back_hidden = lax.dot_general(
        scaled_flat, down_e, (((1,), (1,)), ((), ())), preferred_element_type=jnp.float32
    )
    return (back_hidden * factor).astype(jnp.bfloat16)


def send_back(term_block):
    return lax.all_to_all(term_block, "expert", split_axis=0, concat_axis=0, tiled=True)


def per_device(tokens, cotangent, expert_ids, combine, w_gate, w_up, w_down, tangent_gate):
    expert_count = lax.axis_size("expert")
    rows_dev, top_count = expert_ids.shape
    model_width = tokens.shape[1]
    capacity = rows_dev * top_count * 9 // (8 * expert_count)
    owners = jnp.arange(expert_count, dtype=jnp.int32)
    matches = (expert_ids[:, :, None] == owners[None, None, :]).astype(jnp.int32)
    named_count = jnp.sum(matches, axis=1)
    before = jnp.cumsum(named_count, axis=0) - named_count
    slot_pos = jnp.sum(before[:, None, :] * matches, axis=2)
    target = (expert_ids * capacity + slot_pos).reshape(-1)
    spread = jnp.broadcast_to(tokens[:, None, :], (rows_dev, top_count, model_width)).reshape(
        -1, model_width
    )
    scaled = (combine[:, :, None] * cotangent[:, None, :].astype(jnp.float32)).astype(jnp.bfloat16)
    scaled = scaled.reshape(-1, model_width)
    empty = jnp.zeros((expert_count * capacity, model_width), jnp.bfloat16)
    send_rows = empty.at[target].set(spread).reshape(expert_count, capacity, model_width)
    send_scaled = empty.at[target].set(scaled).reshape(expert_count, capacity, model_width)
    gate_e = w_gate[0]
    up_e = w_up[0]
    down_e = w_down[0]
    tangent_e = tangent_gate[0]
    recv_rows, recv_scaled = (
        lax.all_to_all(send_rows, "expert", split_axis=0, concat_axis=0, tiled=True),
        lax.all_to_all(send_scaled, "expert", split_axis=0, concat_axis=0, tiled=True),
    )
    rows_flat = recv_rows.reshape(-1, model_width)
    term, factor = forward_part(rows_flat, gate_e, up_e, down_e, tangent_e)
    returned = send_back(term.reshape(expert_count, capacity, model_width))
    coeff = backward_part(recv_scaled.reshape(-1, model_width), down_e, factor)
    partial_hvp = lax.dot_general(
        rows_flat, coeff, (((0,), (0,)), ((), ())), preferred_element_type=jnp.float32
    )
    hvp_gate = lax.psum_scatter(partial_hvp, "dp", scatter_dimension=0, tiled=True)
    returned_flat = returned.reshape(-1, model_width)
    picked = returned_flat[target].reshape(rows_dev, top_count, model_width)
    output_tangent = jnp.sum(combine[:, :, None] * picked.astype(jnp.float32), axis=1).astype(
        jnp.bfloat16
    )
    return (hvp_gate[None], output_tangent)


def solution(mesh):
    placed = (
        P(("dp", "expert"), None),
        P(("dp", "expert"), None),
        P(("dp", "expert"), None),
        P(("dp", "expert"), None),
        P("expert", None, None),
        P("expert", None, None),
        P("expert", None, None),
        P("expert", None, None),
    )
    return jax.shard_map(
        per_device,
        mesh=mesh,
        in_specs=placed,
        out_specs=(P("expert", "dp", None), P(("dp", "expert"), None)),
        check_vma=False,
    )
```

profile of v0, /device:TPU:13, one launch (start us, length us, event | category | flops | bytes accessed | tf_op | source)
XLA Modules:
  0.0 373.6 jit_solution(7447867122267737855)
XLA Ops:
  7.2 0.0 copy-start
  7.2 0.9 convert_reduce_fusion
  8.0 0.1 copy.16
  8.1 0.2 reduce_window_sum.11
  8.3 0.1 copy.18
  8.4 0.7 select_reduce_fusion
  9.1 0.7 multiply_add_fusion
  9.8 0.1 copy.19
  9.9 0.1 reshape.77
  10.0 9.8 %scatter_custom_fusion = bf16[1152,2048]{1,0:T(8,128)(2,1)} fusion(s32[1024]{0:T(1024)S(1)} %bitcast.45, bf16[]{:T(256)} %constant.7.clone.1, bf16[128,2048]{1,0:T(8,128)(2,1)} %param.8), kind=kCustom, calls=%fused_computation.9 | custom fusion | bytes 5242882 | tf_op jit(solution)/shard_map/scatter | solution.py:52
  19.8 6.7 %all-to-all-start = ((bf16[16,72,2048]{2,1,0:T(8,128)(2,1)}), bf16[16,72,2048]{2,1,0:T(8,128)(2,1)}, u32[]{:S(2)}, u32[]{:S(2)}) async-start(bf16[16,72,2048]{2,1,0:T(8,128)(2,1)} %bitcast.43), calls=%async_computation | async-start | bytes 9437184 | tf_op jit(solution)/shard_map/all_to_all | solution.py:59
  26.5 0.0 copy-done.1
  26.5 0.1 copy.20
  26.6 0.1 mul.77
  26.7 1.1 convert_element_type.30
  27.9 9.8 %scatter_custom_fusion.1 = bf16[1152,2048]{1,0:T(8,128)(2,1)} fusion(s32[1024]{0:T(1024)S(1)} %bitcast.46, f32[128,2048]{1,0:T(8,128)S(1)} %convert_element_type.30, f32[1024]{0:T(1024)S(1)} %mul.77, bf16[]{:T(256)} %constant.7.clone.1), kind=kCustom, calls=%fused_computation.8 | custom fusion | flops 4194304 | bytes 5771266 | tf_op jit(solution)/shard_map/scatter | solution.py:53
  37.7 92.5 %all-to-all-done = bf16[16,72,2048]{2,1,0:T(8,128)(2,1)} async-done(((bf16[16,72,2048]{2,1,0:T(8,128)(2,1)}), bf16[16,72,2048]{2,1,0:T(8,128)(2,1)}, u32[]{:S(2)}, u32[]{:S(2)}) %all-to-all-start) | async-done | bytes 4718624 | tf_op jit(solution)/shard_map/all_to_all | solution.py:59
  130.2 5.1 %all-to-all-start.1 = ((bf16[16,72,2048]{2,1,0:T(8,128)(2,1)}), bf16[16,72,2048]{2,1,0:T(8,128)(2,1)}, u32[]{:S(2)}, u32[]{:S(2)}) async-start(bf16[16,72,2048]{2,1,0:T(8,128)(2,1)} %bitcast.42), calls=%async_computation.1 | async-start | bytes 9437184 | tf_op jit(solution)/shard_map/all_to_all | solution.py:60
  135.3 5.2 %fusion.19 = f32[1152,512]{1,0:T(8,128)S(1)} fusion(bf16[1152,2048]{1,0:T(8,128)(2,1)} %bitcast.3, bf16[1,2048,512]{2,1,0:T(8,128)(2,1)} %param.15), kind=kOutput, calls=%fused_computation.28 | convolution fusion | flops 2415919104 | bytes 9175040 | tf_op jit(solution)/shard_map/dot_general | solution.py:17
  140.6 0.0 copy-start.3
  140.6 5.3 %fusion.21 = f32[1152,512]{1,0:T(8,128)S(1)} fusion(bf16[1152,2048]{1,0:T(8,128)(2,1)} %bitcast.3, bf16[1,2048,512]{2,1,0:T(8,128)(2,1)S(1)} %copy-done.2), kind=kOutput, calls=%fused_computation.30 | convolution fusion | flops 2415919104 | bytes 9175040 | tf_op jit(solution)/shard_map/dot_general | solution.py:15
  145.9 5.3 %fusion.23 = f32[1152,512]{1,0:T(8,128)S(1)} fusion(bf16[1152,2048]{1,0:T(8,128)(2,1)} %bitcast.3, bf16[1,2048,512]{2,1,0:T(8,128)(2,1)S(1)} %copy-done.3), kind=kOutput, calls=%fused_computation.32 | convolution fusion | flops 2415919104 | bytes 9175040 | tf_op jit(solution)/shard_map/dot_general | solution.py:16
  151.3 1.5 copy-done.6
  152.8 4.9 %convolution_convert_fusion = bf16[1152,2048]{1,0:T(8,128)(2,1)} fusion(bf16[1,512,2048]{2,1,0:T(8,128)(2,1)S(1)} %copy-done, f32[1152,512]{1,0:T(8,128)S(1)} %fusion.23, f32[1152,512]{1,0:T(8,128)S(1)} %fusion.19, f32[1152,512]{1,0:T(8,128)S(1)} %fusion.21), kind=kOutput, calls=%fused_computation.7 | convolution fusion | flops 2424176640 | bytes 13893632 | tf_op jit(solution)/shard_map/dot_general | solution.py:20
  157.7 81.3 %all-to-all-done.1 = bf16[16,72,2048]{2,1,0:T(8,128)(2,1)} async-done(((bf16[16,72,2048]{2,1,0:T(8,128)(2,1)}), bf16[16,72,2048]{2,1,0:T(8,128)(2,1)}, u32[]{:S(2)}, u32[]{:S(2)}) %all-to-all-start.1) | async-done | bytes 4718624 | tf_op jit(solution)/shard_map/all_to_all | solution.py:60
  239.0 4.9 %all-to-all-start.2 = ((bf16[16,72,2048]{2,1,0:T(8,128)(2,1)}), bf16[16,72,2048]{2,1,0:T(8,128)(2,1)}, u32[]{:S(2)}, u32[]{:S(2)}) async-start(bf16[16,72,2048]{2,1,0:T(8,128)(2,1)} %bitcast.44), calls=%async_computation.3 | async-start | bytes 9437184 | tf_op jit(solution)/shard_map/all_to_all | solution.py:32
  243.9 0.0 reduce-scatter.2.cloned.1.call-start
  244.0 14.0 %fusion.31 = f32[2048,512]{1,0:T(8,128)} fusion(bf16[1152,2048]{1,0:T(8,128)(2,1)} %bitcast.3, bf16[1152,2048]{1,0:T(8,128)(2,1)} %bitcast.6, f32[1152,512]{1,0:T(8,128)} %copy-done.4, f32[1152,512]{1,0:T(8,128)} %copy-done.6, f32[1152,512]{1,0:T(8,128)} %copy-done.5, bf16[1,512,2048]{2,1,0:T(8,128)(2,1)S(1)} %copy-done), kind=kOutput, calls=%fused_computation.42 | convolution fusion | flops 4840095744 | bytes 22806528 | tf_op jit(solution)/shard_map/dot_general | solution.py:66
  258.0 0.0 reduce-scatter.2.cloned.1.call-update
  258.0 89.6 %all-to-all-done.2 = bf16[16,72,2048]{2,1,0:T(8,128)(2,1)} async-done(((bf16[16,72,2048]{2,1,0:T(8,128)(2,1)}), bf16[16,72,2048]{2,1,0:T(8,128)(2,1)}, u32[]{:S(2)}, u32[]{:S(2)}) %all-to-all-start.2) | async-done | bytes 4718624 | tf_op jit(solution)/shard_map/all_to_all | solution.py:32
  347.6 11.8 %gather_fusion = bf16[1024,2048]{1,0:T(8,128)(2,1)} fusion(bf16[1152,2048]{1,0:T(8,128)(2,1)} %bitcast.13, s32[1024]{0:T(1024)S(1)} %broadcast_clamp_fusion), kind=kCustom, calls=%fused_computation | custom fusion | bytes 8392704 | tf_op jit(solution)/shard_map/gather | solution.py:71
  359.4 7.3 %fusion = bf16[128,2048]{1,0:T(8,128)(2,1)} fusion(bf16[1024,2048]{1,0:T(8,128)(2,1)} %gather_fusion, f32[128,8]{1,0:T(8,128)S(1)} %copy.20), kind=kLoop, calls=%fused_computation.4 | loop fusion | flops 6029312 | bytes 4722688 | tf_op jit(solution)/shard_map/reduce_sum | solution.py:72
  (14 shorter events, 0.0 us)
Async XLA Ops:
  7.2 145.6 %copy-start = (bf16[1,512,2048]{2,1,0:T(8,128)(2,1)S(1)}, bf16[1,512,2048]{2,1,0:T(8,128)(2,1)}, u32[]{:S(2)}) copy-start(bf16[1,512,2048]{2,1,0:T(8,128)(2,1)} %param.14) | copy-start | bytes 6291460
  19.8 6.7 %copy-start.1 = (f32[128,8]{0,1:T(8,128)S(1)}, f32[128,8]{0,1:T(8,128)}, u32[]{:S(2)}) copy-start(f32[128,8]{0,1:T(8,128)} %param.11) | copy-start | bytes 12292
  19.8 110.4 %all-to-all-start = ((bf16[16,72,2048]{2,1,0:T(8,128)(2,1)}), bf16[16,72,2048]{2,1,0:T(8,128)(2,1)}, u32[]{:S(2)}, u32[]{:S(2)}) async-start(bf16[16,72,2048]{2,1,0:T(8,128)(2,1)} %bitcast.43), calls=%async_computation | async-start | bytes 9437184 | tf_op jit(solution)/shard_map/all_to_all | solution.py:59
  130.2 108.8 %all-to-all-start.1 = ((bf16[16,72,2048]{2,1,0:T(8,128)(2,1)}), bf16[16,72,2048]{2,1,0:T(8,128)(2,1)}, u32[]{:S(2)}, u32[]{:S(2)}) async-start(bf16[16,72,2048]{2,1,0:T(8,128)(2,1)} %bitcast.42), calls=%async_computation.1 | async-start | bytes 9437184 | tf_op jit(solution)/shard_map/all_to_all | solution.py:60
  135.3 5.3 %copy-start.2 = (bf16[1,2048,512]{2,1,0:T(8,128)(2,1)S(1)}, bf16[1,2048,512]{2,1,0:T(8,128)(2,1)}, u32[]{:S(2)}) copy-start(bf16[1,2048,512]{2,1,0:T(8,128)(2,1)} %param.12) | copy-start | bytes 6291460
  140.6 10.7 %copy-start.4 = (f32[1152,512]{1,0:T(8,128)}, f32[1152,512]{1,0:T(8,128)S(1)}, u32[]{:S(2)}) copy-start(f32[1152,512]{1,0:T(8,128)S(1)} %fusion.19) | copy-start | bytes 7077892
  140.6 5.4 %copy-start.3 = (bf16[1,2048,512]{2,1,0:T(8,128)(2,1)S(1)}, bf16[1,2048,512]{2,1,0:T(8,128)(2,1)}, u32[]{:S(2)}) copy-start(bf16[1,2048,512]{2,1,0:T(8,128)(2,1)} %param.13) | copy-start | bytes 6291460
  145.9 5.3 %copy-start.5 = (f32[1152,512]{1,0:T(8,128)}, f32[1152,512]{1,0:T(8,128)S(1)}, u32[]{:S(2)}) copy-start(f32[1152,512]{1,0:T(8,128)S(1)} %fusion.21) | copy-start | bytes 7077892
  151.3 1.5 copy-start.6
  239.0 108.6 %all-to-all-start.2 = ((bf16[16,72,2048]{2,1,0:T(8,128)(2,1)}), bf16[16,72,2048]{2,1,0:T(8,128)(2,1)}, u32[]{:S(2)}, u32[]{:S(2)}) async-start(bf16[16,72,2048]{2,1,0:T(8,128)(2,1)} %bitcast.44), calls=%async_computation.3 | async-start | bytes 9437184 | tf_op jit(solution)/shard_map/all_to_all | solution.py:32
  243.9 122.8 %reduce-scatter.2.cloned.1.call-start = ((), (), s32[]{:S(2)}) async-start(), calls=%async_computation.4 | async-start | bytes 6291456 | tf_op jit(solution)/shard_map/reduce_scatter | solution.py:69
Sparse Core Ops, SparseCore 0:
  258.1 54.8 reduce-scatter.1
where the time goes:
time: 374 us
  waiting for transfers between devices  263 us (70%)
  matrix products  34.8 us (9%)
  local copies, waits for them, and re-layouts  23.6 us (6%)
  other arithmetic  20.8 us (6%)
  starting transfers between devices  16.7 us (4%)
  between operations  14.2 us (4%)
    all_to_all x1, waiting for transfers between devices, per_device(): lax.all_to_all(send_rows, 'expert', split_axis=0, concat_axis=0, tiled=True)  92.5 us
    all_to_all x1, waiting for transfers between devices, send_back(): lax.all_to_all(term_block, 'expert', split_axis=0, concat_axis=0, tiled=T...  89.6 us
    all_to_all x1, waiting for transfers between devices, per_device(): lax.all_to_all(send_scaled, 'expert', split_axis=0, concat_axis=0, tiled=...  81.3 us
    dot_general x1, matrix products, per_device(): lax.dot_general(rows_flat, coeff, (((0,), (0,)), ((), ())), preferred_ele...  14 us
    gather x1, local copies, waits for them, and re-layouts, per_device(): picked = returned_flat[target].reshape(rows_dev, top_count, model_width)  11.8 us
    scatter x1, other arithmetic, per_device(): empty.at[target].set(scaled).reshape(expert_count, capacity, model_width)  9.83 us
    scatter x1, local copies, waits for them, and re-layouts, per_device(): empty.at[target].set(spread).reshape(expert_count, capacity, model_width)  9.81 us
  transfers between devices with their start and end apart: 4, of which 3 were waited for; matrix products, arithmetic and copies ran while one was open for 17% of the time, Pallas kernels for 0%

commit v1 on v0

v1 whole, which is shorter than its diff:
```python
import jax
import jax.numpy as jnp
from jax import lax
from jax.sharding import PartitionSpec as P


def silu_derivs(gate_act):
    squash = jax.nn.sigmoid(gate_act)
    first = squash * (1.0 + gate_act * (1.0 - squash))
    second = squash * (1.0 - squash) * (2.0 + gate_act * (1.0 - 2.0 * squash))
    return (first, second)


def weight_table(expert_ids, combine, expert_count):
    owners = jnp.arange(expert_count, dtype=jnp.int32)
    chosen = expert_ids[:, :, None] == owners[None, None, :]
    return jnp.sum(jnp.where(chosen, combine[:, :, None], 0.0), axis=1).T


def per_device(tokens, cotangent, expert_ids, combine, w_gate, w_up, w_down, tangent_gate):
    expert_count = lax.axis_size("expert")
    rows_dev, top_count = expert_ids.shape
    model_width = tokens.shape[1]
    capacity = rows_dev * top_count * 9 // (8 * expert_count)
    table = weight_table(expert_ids, combine, expert_count)
    weights = lax.all_to_all(table, "expert", split_axis=0, concat_axis=0, tiled=True)
    tokens_all = lax.all_gather(tokens, "expert", axis=0)
    cotangent_all = lax.all_gather(cotangent, "expert", axis=0)
    present = weights > 0.0
    counted = present.astype(jnp.int32)
    position = jnp.cumsum(counted, axis=1) - counted
    slots = jnp.arange(capacity, dtype=jnp.int32)
    hit = (position[:, None, :] == slots[None, :, None]) & present[:, None, :]
    select = hit.astype(jnp.bfloat16)
    slot_weight = jnp.sum(jnp.where(hit, weights[:, None, :], 0.0), axis=2).reshape(-1, 1)

    def pick(block):
        out = jnp.einsum("scr,srd->scd", select, block, preferred_element_type=jnp.float32)
        return out.reshape(-1, model_width)

    rows_flat = pick(tokens_all).astype(jnp.bfloat16)
    gate_act = jnp.dot(rows_flat, w_gate[0], preferred_element_type=jnp.float32)
    up_act = jnp.dot(rows_flat, w_up[0], preferred_element_type=jnp.float32)
    gate_dot = jnp.dot(rows_flat, tangent_gate[0], preferred_element_type=jnp.float32)
    first, second = silu_derivs(gate_act)
    lifted = (first * gate_dot * up_act).astype(jnp.bfloat16)
    term = jnp.dot(lifted, w_down[0], preferred_element_type=jnp.float32)
    weighted = (slot_weight * term).astype(jnp.bfloat16).reshape(expert_count, capacity, model_width)
    partial = jnp.einsum("scr,scd->srd", select, weighted, preferred_element_type=jnp.float32)
    partial = partial.astype(jnp.bfloat16).reshape(-1, model_width)
    output_tangent = lax.psum_scatter(partial, "expert", scatter_dimension=0, tiled=True)
    scaled = (slot_weight * pick(cotangent_all)).astype(jnp.bfloat16)
    back_hidden = lax.dot_general(
        scaled, w_down[0], (((1,), (1,)), ((), ())), preferred_element_type=jnp.float32
    )
    coeff = (back_hidden * (up_act * second * gate_dot)).astype(jnp.bfloat16)
    partial_hvp = lax.dot_general(
        rows_flat, coeff, (((0,), (0,)), ((), ())), preferred_element_type=jnp.float32
    )
    hvp_gate = lax.psum_scatter(partial_hvp, "dp", scatter_dimension=0, tiled=True)
    return (hvp_gate[None], output_tangent)


def solution(mesh):
    rows = P(("dp", "expert"), None)
    owned = P("expert", None, None)
    return jax.shard_map(
        per_device,
        mesh=mesh,
        in_specs=(rows, rows, rows, rows, owned, owned, owned, owned),
        out_specs=(P("expert", "dp", None), rows),
        check_vma=False,
    )
```

time: 374 us -> 353 us (0.944)
  local copies, waits for them, and re-layouts: 23.6 us -> 0.11 us
  other arithmetic: 20.8 us -> 1.38 us
  starting transfers between devices: 16.7 us -> 0.16 us
  matrix products: 34.8 us -> 50.1 us
  waiting for transfers between devices: 263 us -> 276 us
  blocking collectives: 0 us -> 10.2 us
    all_to_all x3 -> x0, waiting for transfers between devices: 263 us -> none  [the longest x1 92.5 us: per_device(): lax.all_to_all(send_rows, 'expert', split_axis=0, concat_axis=0, tiled=True)]
    all_gather x0 -> x2, waiting for transfers between devices: none -> 123 us  [the longest x1 64.9 us: per_device(): tokens_all = lax.all_gather(tokens, 'expert', axis=0)]
    reduce_scatter x0 -> x1, waiting for transfers between devices: none -> 110 us  [per_device(): lax.psum_scatter(partial, 'expert', scatter_dimension=0, tiled=True)]
    reduce_scatter x1, waiting for transfers between devices: 0.01 us -> 41.7 us  [per_device(): lax.psum_scatter(partial_hvp, 'dp', scatter_dimension=0, tiled=True)]
    all_to_all x3 -> x0, starting transfers between devices: 16.7 us -> none  [the longest x1 6.69 us: per_device(): lax.all_to_all(send_rows, 'expert', split_axis=0, concat_axis=0, tiled=True)]
    dot_general x4 -> x7, matrix products: 20.8 us -> 35.8 us  [the longest x2 11.8 us: pick(): jnp.einsum('scr,srd->scd', select, block, preferred_element_type=jnp.floa...]
    gather x1 -> x0, local copies, waits for them, and re-layouts: 11.8 us -> none  [per_device(): picked = returned_flat[target].reshape(rows_dev, top_count, model_width)]
    all_to_all x0 -> x1, blocking collectives: none -> 10.2 us  [per_device(): lax.all_to_all(table, 'expert', split_axis=0, concat_axis=0, tiled=True)]
  transfers between devices with their start and end apart: 4 -> 4, of which waited for: 3 -> 4; matrix products, arithmetic and copies ran while one was open for 17% -> 9% of each run, Pallas kernels for 0% -> 0%
where the time goes in v1:
time: 353 us; the launch traced here: 352 us
  waiting for transfers between devices  276 us (78%)
  matrix products  50.1 us (14%)
  between operations  13.8 us (4%)
  blocking collectives  10.2 us (3%)
    reduce_scatter x1, waiting for transfers between devices, per_device(): lax.psum_scatter(partial, 'expert', scatter_dimension=0, tiled=True)  110 us
    all_gather x1, waiting for transfers between devices, per_device(): tokens_all = lax.all_gather(tokens, 'expert', axis=0)  64.9 us
    all_gather x1, waiting for transfers between devices, per_device(): cotangent_all = lax.all_gather(cotangent, 'expert', axis=0)  58.3 us
    reduce_scatter x1, waiting for transfers between devices, per_device(): lax.psum_scatter(partial_hvp, 'dp', scatter_dimension=0, tiled=True)  41.7 us
    dot_general x1, matrix products, per_device(): lax.dot_general(rows_flat, coeff, (((0,), (0,)), ((), ())), preferred_ele...  14.2 us
    dot_general x2, matrix products, pick(): jnp.einsum('scr,srd->scd', select, block, preferred_element_type=jnp.floa...  11.8 us
    all_to_all x1, blocking collectives, per_device(): lax.all_to_all(table, 'expert', split_axis=0, concat_axis=0, tiled=True)  10.2 us
  transfers between devices with their start and end apart: 4, of which 4 were waited for; matrix products, arithmetic and copies ran while one was open for 9% of the time, Pallas kernels for 0%

profile of v1, /device:TPU:13, one launch (start us, length us, event | category | flops | bytes accessed | tf_op | source)
XLA Modules:
  0.0 351.7 jit_solution(4328936507722670280)
XLA Ops:
  7.2 0.0 copy-start
  7.2 0.0 all-gather.5.cloned.1.call-start
  7.2 0.7 all-gather.5.cloned.1.call-update
  7.9 0.0 all-gather.7.cloned.1.call-start
  8.0 0.7 all-gather.7.cloned.1.call-update
  8.7 0.0 reduce-scatter.3.cloned.1.call-start
  8.7 0.7 select_reduce_fusion.1
  9.4 10.2 %all_to_all.12 = f32[16,1,128]{2,1,0:T(1,128)S(1)} all-to-all(f32[16,1,128]{2,1,0:T(1,128)S(1)} %bitcast.56), channel_id=1, replica_groups=mesh['dp'=2,'expert'=16] {'expert'}, dimensions={0} | all-to-all | bytes 16384 | tf_op jit(solution)/shard_map/all_to_all | solution.py:26
  19.6 0.3 reduce_window_sum.11
  19.9 0.4 select_reduce_fusion
  20.2 64.9 %all-gather.5.cloned.1.call-done = bf16[2048,2048]{1,0:T(8,128)(2,1)} async-done(((bf16[128,2048]{1,0:T(8,128)(2,1)}), bf16[2048,2048]{1,0:T(8,128)(2,1)}) %all-gather.5.cloned.1.call-update) | async-done | bytes 8388624 | tf_op jit(solution)/shard_map/all_gather | solution.py:27
  85.1 4.9 %convolution_convert_fusion.1 = bf16[16,72,2048]{2,1,0:T(8,128)(2,1)S(1)} fusion(bf16[16,128,2048]{2,1,0:T(8,128)(2,1)} %bitcast.43, s32[16,128]{1,0:T(8,128)S(1)} %subtract_bitcast_fusion, pred[16,128]{1,0:T(8,128)(4,1)S(1)} %bitcast.51), kind=kOutput, calls=%fused_computation.4 | convolution fusion | flops 606633984 | bytes 13117440 | tf_op jit(solution)/shard_map/scr,srd->scd/dot_general | solution.py:38
  90.0 0.0 copy-start.1
  90.0 0.0 copy-done.2
  90.1 0.0 copy-start.3
  90.1 4.0 %fusion.10 = f32[1152,512]{1,0:T(8,128)} fusion(bf16[1152,2048]{1,0:T(8,128)(2,1)S(1)} %bitcast.45, bf16[1,2048,512]{2,1,0:T(8,128)(2,1)S(1)} %copy-done.2), kind=kOutput, calls=%fused_computation.18 | convolution fusion | flops 2415919104 | bytes 9175040 | tf_op jit(solution)/shard_map/dot_general | solution.py:44
  94.1 0.0 copy-done.3
  94.1 4.0 %fusion.14 = f32[1152,512]{1,0:T(8,128)} fusion(bf16[1152,2048]{1,0:T(8,128)(2,1)S(1)} %bitcast.46, bf16[1,2048,512]{2,1,0:T(8,128)(2,1)S(1)} %copy-done.3), kind=kOutput, calls=%fused_computation.22 | convolution fusion | flops 2415919104 | bytes 9175040 | tf_op jit(solution)/shard_map/dot_general | solution.py:43
  98.1 0.0 copy-done.1
  98.1 0.0 copy-done.4
  98.1 4.1 %fusion.12 = f32[1152,512]{1,0:T(8,128)} fusion(bf16[1152,2048]{1,0:T(8,128)(2,1)S(1)} %bitcast.47, bf16[1,2048,512]{2,1,0:T(8,128)(2,1)S(1)} %copy-done.4), kind=kOutput, calls=%fused_computation.20 | convolution fusion | flops 2415919104 | bytes 9175040 | tf_op jit(solution)/shard_map/dot_general | solution.py:42
  102.2 58.3 %all-gather.7.cloned.1.call-done = bf16[2048,2048]{1,0:T(8,128)(2,1)} async-done(((bf16[128,2048]{1,0:T(8,128)(2,1)}), bf16[2048,2048]{1,0:T(8,128)(2,1)}) %all-gather.7.cloned.1.call-update) | async-done | bytes 8388624 | tf_op jit(solution)/shard_map/all_gather | solution.py:28
  160.5 6.9 %multiply_convert_fusion = bf16[16,72,2048]{2,1,0:T(8,128)(2,1)} fusion(f32[16,72]{1,0:T(8,128)S(1)} %select_reduce_fusion, bf16[16,128,2048]{2,1,0:T(8,128)(2,1)} %bitcast.42, s32[16,128]{1,0:T(8,128)S(1)} %subtract_bitcast_fusion, pred[16,128]{1,0:T(8,128)(4,1)S(1)} %bitcast.52), kind=kOutput, calls=%fused_computation.1 | convolution fusion | flops 608993280 | bytes 13122048 | tf_op jit(solution)/shard_map/scr,srd->scd/dot_general | solution.py:38
  167.3 14.2 %fusion.31 = f32[2048,512]{1,0:T(8,128)} fusion(bf16[1152,2048]{1,0:T(8,128)(2,1)} %bitcast.48, bf16[1152,2048]{1,0:T(8,128)(2,1)} %bitcast.44, f32[1152,512]{1,0:T(8,128)} %fusion.10, f32[1152,512]{1,0:T(8,128)} %fusion.14, f32[1152,512]{1,0:T(8,128)} %fusion.12, bf16[1,512,2048]{2,1,0:T(8,128)(2,1)S(1)} %copy-done), kind=kOutput, calls=%fused_computation.38 | convolution fusion | flops 4840095744 | bytes 22806528 | tf_op jit(solution)/shard_map/dot_general | solution.py:57
  181.6 0.0 reduce-scatter.3.cloned.1.call-update
  181.6 0.0 reduce-scatter.5.cloned.1.call-start
  181.6 0.1 mul.61
  181.7 6.2 %fusion = bf16[1152,2048]{1,0:T(8,128)(2,1)S(1)} fusion(f32[1152]{0:T(1024)S(1)} %mul.61, bf16[1,512,2048]{2,1,0:T(8,128)(2,1)S(1)} %copy-done, f32[1152,512]{1,0:T(8,128)} %fusion.14, f32[1152,512]{1,0:T(8,128)} %fusion.10, f32[1152,512]{1,0:T(8,128)} %fusion.12), kind=kOutput, calls=%fused_computation.2 | convolution fusion | flops 2426535936 | bytes 13898240 | tf_op jit(solution)/shard_map/dot_general | solution.py:47
  187.9 5.8 %convolution_convert_fusion = bf16[16,128,2048]{2,1,0:T(8,128)(2,1)} fusion(bf16[16,72,2048]{2,1,0:T(8,128)(2,1)S(1)} %bitcast.49, s32[16,128]{1,0:T(8,128)S(1)} %subtract_bitcast_fusion, pred[16,128]{1,0:T(8,128)(4,1)S(1)} %bitcast.53), kind=kOutput, calls=%fused_computation.3 | convolution fusion | flops 608468992 | bytes 13117440 | tf_op jit(solution)/shard_map/scr,scd->srd/dot_general | solution.py:49
  193.7 0.0 reduce-scatter.5.cloned.1.call-update
  193.7 41.7 %reduce-scatter.3.cloned.1.call-done = f32[1024,512]{1,0:T(8,128)} async-done(((f32[2048,512]{1,0:T(8,128)}), f32[1024,512]{1,0:T(8,128)}) %reduce-scatter.3.cloned.1.call-update) | async-done | bytes 2097168 | tf_op jit(solution)/shard_map/reduce_scatter | solution.py:60
  235.4 109.7 %reduce-scatter.5.cloned.1.call-done = bf16[128,2048]{1,0:T(8,128)(2,1)} async-done(((bf16[2048,2048]{1,0:T(8,128)(2,1)}), bf16[128,2048]{1,0:T(8,128)(2,1)}) %reduce-scatter.5.cloned.1.call-update) | async-done | bytes 524304 | tf_op jit(solution)/shard_map/reduce_scatter | solution.py:51
  (5 shorter events, 0.0 us)
Async XLA Ops:
  7.2 160.2 %copy-start = (bf16[1,512,2048]{2,1,0:T(8,128)(2,1)S(1)}, bf16[1,512,2048]{2,1,0:T(8,128)(2,1)}, u32[]{:S(2)}) copy-start(bf16[1,512,2048]{2,1,0:T(8,128)(2,1)} %param.14) | copy-start | bytes 6291460
  7.2 77.9 %all-gather.5.cloned.1.call-start = ((), (), s32[]{:S(2)}) async-start(), calls=%async_computation.5 | async-start | bytes 8912896 | tf_op jit(solution)/shard_map/all_gather | solution.py:27
  7.9 152.6 %all-gather.7.cloned.1.call-start = ((), (), s32[]{:S(2)}) async-start(), calls=%async_computation.6 | async-start | bytes 8912896 | tf_op jit(solution)/shard_map/all_gather | solution.py:28
  8.7 226.8 %reduce-scatter.3.cloned.1.call-start = ((), (), s32[]{:S(2)}) async-start(), calls=%async_computation.3 | async-start | bytes 6291456 | tf_op jit(solution)/shard_map/reduce_scatter | solution.py:60
  85.1 4.9 %copy-start.2 = (bf16[1,2048,512]{2,1,0:T(8,128)(2,1)S(1)}, bf16[1,2048,512]{2,1,0:T(8,128)(2,1)}, u32[]{:S(2)}) copy-start(bf16[1,2048,512]{2,1,0:T(8,128)(2,1)} %param.15) | copy-start | bytes 6291460
  90.0 8.1 %copy-start.1 = (bf16[16,72,2048]{2,1,0:T(8,128)(2,1)}, bf16[16,72,2048]{2,1,0:T(8,128)(2,1)S(1)}, u32[]{:S(2)}) copy-start(bf16[16,72,2048]{2,1,0:T(8,128)(2,1)S(1)} %convolution_convert_fusion.1) | copy-start | bytes 14155780
  90.1 4.1 %copy-start.3 = (bf16[1,2048,512]{2,1,0:T(8,128)(2,1)S(1)}, bf16[1,2048,512]{2,1,0:T(8,128)(2,1)}, u32[]{:S(2)}) copy-start(bf16[1,2048,512]{2,1,0:T(8,128)(2,1)} %param.13) | copy-start | bytes 6291460
  94.1 4.0 %copy-start.4 = (bf16[1,2048,512]{2,1,0:T(8,128)(2,1)S(1)}, bf16[1,2048,512]{2,1,0:T(8,128)(2,1)}, u32[]{:S(2)}) copy-start(bf16[1,2048,512]{2,1,0:T(8,128)(2,1)} %param.12) | copy-start | bytes 6291460
  181.6 163.6 %reduce-scatter.5.cloned.1.call-start = ((), (), s32[]{:S(2)}) async-start(), calls=%async_computation.4 | async-start | bytes 8912896 | tf_op jit(solution)/shard_map/reduce_scatter | solution.py:51
Sparse Core Ops, SparseCore 0:
  10.2 74.9 all-gather.4
  87.3 73.1 all-gather.6
  181.7 53.6 reduce-scatter.2
  240.5 104.6 reduce-scatter.4

commit v2 on v1

--- a/solution.py
+++ b/solution.py
@@ -1,6 +1,9 @@
+import functools
 import jax
 import jax.numpy as jnp
 from jax import lax
+from jax.experimental import pallas as pl
+from jax.experimental.pallas import tpu as pltpu
 from jax.sharding import PartitionSpec as P
 
 
@@ -17,7 +20,7 @@
     return jnp.sum(jnp.where(chosen, combine[:, :, None], 0.0), axis=1).T
 
 
-def per_device(tokens, cotangent, expert_ids, combine, w_gate, w_up, w_down, tangent_gate):
+def gathered(tokens, cotangent, expert_ids, combine, w_gate, w_up, w_down, tangent_gate):
     expert_count = lax.axis_size("expert")
     rows_dev, top_count = expert_ids.shape
     model_width = tokens.shape[1]
@@ -61,6 +64,284 @@
     return (hvp_gate[None], output_tangent)
 
 
+NZ, NY, NC = 4, 2, 2
+
+
+def kernel(
+    capacity,
+    table_ref, tokens_ref, cot_ref, gate_ref, up_ref, down_ref, tan_ref,
+    hvp_ref, out_ref,
+    table, tok, cot, rows, factor, coeff, part, sib_in, y_in, z_in, x_out, x_in,
+    g_send, g_recv, s_send, s_recv, y_send, y_recv, z_send, z_recv, x_send, x_recv,
+):
+    f32, b16 = jnp.float32, jnp.bfloat16
+    dp, me = lax.axis_index("dp"), lax.axis_index("expert")
+    c, y, z = me % NC, (me // NC) % NY, me // (NC * NY)
+    n = tokens_ref.shape[0]
+    pairs = NZ * NY
+    height = NC * capacity
+    half = hvp_ref.shape[0]
+
+    def at(zz, yy, cc):
+        return (zz * NY + yy) * NC + cc
+
+    def zj(j):
+        return (z + j) % NZ
+
+    def yj(j):
+        return (y + j // NZ) % NY
+
+    sibling, across = at(z, y, 1 - c), at(z, 1 - y, c)
+    other = (1 - dp, me)
+    peers = [(dp, sibling), (dp, across), other] + [(dp, at(zj(j), y, c)) for j in range(1, NZ)]
+    barrier = pltpu.get_barrier_semaphore()
+    for peer in peers:
+        pl.semaphore_signal(barrier, inc=1, device_id=peer, device_id_type=pl.DeviceIdType.MESH)
+    pl.semaphore_wait(barrier, len(peers))
+
+    def remote(src, dst, send, recv, peer):
+        return pltpu.make_async_remote_copy(
+            src_ref=src, dst_ref=dst, send_sem=send, recv_sem=recv,
+            device_id=peer, device_id_type=pl.DeviceIdType.MESH,
+        )
+
+    sent = []
+
+    def begin(copy):
+        copy.start()
+        sent.append(copy)
+
+    fulls = (table, tok, cot)
+    owns = (table_ref, tokens_ref, cot_ref)
+
+    def piece(a, b):
+        return table.at[b] if a == 0 else fulls[a].at[pl.ds(b * n, n)]
+
+    def send_block(a, src, b, slot, peer):
+        begin(remote(src, piece(a, b), g_send.at[a, slot], g_recv.at[a, b], peer))
+
+    def arrived(a, b):
+        remote(piece(a, b), piece(a, b), g_send.at[a, 0], g_recv.at[a, b], (dp, sibling)).wait_recv()
+
+    def send_own(a):
+        send_block(a, owns[a], me, 0, (dp, across))
+        for j in range(1, NZ):
+            send_block(a, owns[a], me, j, (dp, at(zj(j), y, c)))
+        send_block(a, owns[a], me, NZ, (dp, sibling))
+
+    def pass_row(a, j):
+        b = at(zj(j), y, c)
+        arrived(a, b)
+        send_block(a, piece(a, b), b, NZ + j, (dp, across))
+        send_block(a, piece(a, b), b, 2 * NZ - 1 + j, (dp, sibling))
+
+    def pass_across(a, j):
+        b = at(zj(j), 1 - y, c)
+        arrived(a, b)
+        send_block(a, piece(a, b), b, 3 * NZ - 1 + j, (dp, sibling))
+
+    send_own(0)
+    send_own(1)
+    table[me] = table_ref[...]
+    tok[pl.ds(me * n, n), :] = tokens_ref[...]
+    cot[pl.ds(me * n, n), :] = cot_ref[...]
+    for j in range(1, NZ):
+        pass_row(0, j)
+        pass_row(1, j)
+    send_own(2)
+
+    def choose(j):
+        base = at(zj(j), yj(j), 0)
+        owner = lax.broadcasted_iota(jnp.int32, (table.shape[1], n), 0) == me
+        earlier = lax.broadcasted_iota(jnp.int32, (n, n), 0) < lax.broadcasted_iota(
+            jnp.int32, (n, n), 1
+        )
+        earlier = earlier.astype(f32).astype(b16)
+        weights, places = [], []
+        for cc in range(NC):
+            w = jnp.sum(jnp.where(owner, table[base + cc], 0.0), axis=0, keepdims=True)
+            present = jnp.where(jnp.broadcast_to(w, (16, n)) > 0.0, 1.0, 0.0).astype(b16)
+            place = jnp.dot(present, earlier, preferred_element_type=f32)[0:1, :]
+            weights.append(w)
+            places.append(place + float(cc * capacity))
+        w, place = jnp.concatenate(weights, axis=1), jnp.concatenate(places, axis=1)
+        slot = lax.broadcasted_iota(jnp.int32, (height, NC * n), 0).astype(f32)
+        hit = (slot == place) & (w > 0.0)
+        select = jnp.where(hit, 1.0, 0.0)
+        slot_weight = jnp.sum(jnp.where(hit, w, 0.0), axis=1, keepdims=True)
+        return base, select.astype(b16), slot_weight
+
+    def forward(j0):
+        found = []
+        for k in range(2):
+            base, select, slot_weight = choose(j0 + k)
+            both = tok[pl.ds(base * n, NC * n), :]
+            mine = jnp.dot(select, both, preferred_element_type=f32).astype(b16)
+            rows[pl.ds((j0 + k) * height, height), :] = mine
+            found.append((select, slot_weight))
+        at_rows = pl.ds(j0 * height, 2 * height)
+        held = rows[at_rows, :]
+        gate_act = jnp.dot(held, gate_ref[...], preferred_element_type=f32)
+        up_act = jnp.dot(held, up_ref[...], preferred_element_type=f32)
+        gate_dot = jnp.dot(held, tan_ref[...], preferred_element_type=f32)
+        first, second = silu_derivs(gate_act)
+        factor[at_rows, :] = up_act * second * gate_dot
+        lifted = first * gate_dot * up_act
+        for k in range(2):
+            select, slot_weight = found[k]
+            one = (lifted[k * height:(k + 1) * height] * slot_weight).astype(b16)
+            spread = lax.dot_general(
+                select, one, (((0,), (0,)), ((), ())), preferred_element_type=f32
+            ).astype(b16)
+            part[j0 + k] = jnp.dot(spread, down_ref[...], preferred_element_type=f32).astype(b16)
+
+    def from_sibling(a, j0):
+        for k in range(2):
+            arrived(a, at(zj(j0 + k), yj(j0 + k), 1 - c))
+
+    def to_sibling(j):
+        begin(remote(
+            part.at[j, pl.ds((1 - c) * n, n)], sib_in.at[j], s_send.at[j], s_recv.at[j],
+            (dp, sibling),
+        ))
+
+    def landed(buf, sem):
+        remote(buf, buf, s_send.at[0], sem, (dp, sibling)).wait_recv()
+
+    def group(j0):
+        from_sibling(0, j0)
+        from_sibling(1, j0)
+        forward(j0)
+        to_sibling(j0)
+        to_sibling(j0 + 1)
+
+    group(0)
+    group(2)
+    for j in range(NZ):
+        pass_across(0, j)
+        pass_across(1, j)
+    for j in range(1, NZ):
+        pass_row(2, j)
+    group(4)
+    group(6)
+
+    def own_half(j):
+        return part.at[j, pl.ds(c * n, n)]
+
+    def chip_sum(j):
+        landed(sib_in.at[j], s_recv.at[j])
+        return own_half(j)[...].astype(f32) + sib_in[j].astype(f32)
+
+    for j in (5, 6, 7, 4):
+        own_half(j)[...] = chip_sum(j).astype(b16)
+        begin(remote(own_half(j), y_in.at[j - NZ], y_send.at[j - NZ], y_recv.at[j - NZ], (dp, across)))
+    for j in range(NZ):
+        pass_across(2, j)
+
+    for j0 in range(0, pairs, 2):
+        from_sibling(2, j0)
+        for k in range(2):
+            base, select, slot_weight = choose(j0 + k)
+            both = cot[pl.ds(base * n, NC * n), :]
+            scaled = (slot_weight * jnp.dot(select, both, preferred_element_type=f32)).astype(b16)
+            back = lax.dot_general(
+                scaled, down_ref[...], (((1,), (1,)), ((), ())), preferred_element_type=f32
+            )
+            at_rows = pl.ds((j0 + k) * height, height)
+            coeff[at_rows, :] = (back * factor[at_rows, :]).astype(b16)
+
+    wide = half // 4
+
+    def product(start):
+        cols = rows[:, pl.ds(pl.multiple_of(start, 128), wide)]
+        return lax.dot_general(
+            cols, coeff[...], (((0,), (0,)), ((), ())), preferred_element_type=f32
+        )
+
+    for q in range(4):
+        some = pl.ds(q * wide, wide)
+        x_out[some, :] = product((1 - dp) * half + q * wide).astype(b16)
+        begin(remote(x_out.at[some], x_in.at[some], x_send.at[q], x_recv.at[q], other))
+
+    for j in (1, 2, 3, 0):
+        total = chip_sum(j)
+        landed(y_in.at[j], y_recv.at[j])
+        total = total + y_in[j].astype(f32)
+        own_half(j)[...] = total.astype(b16)
+        if j > 0:
+            begin(remote(
+                own_half(j), z_in.at[j - 1], z_send.at[j - 1], z_recv.at[j - 1],
+                (dp, at(zj(j), y, c)),
+            ))
+    for q in range(4):
+        hvp_ref[pl.ds(q * wide, wide), :] = product(dp * half + q * wide)
+    for q in range(4):
+        some = pl.ds(q * wide, wide)
+        landed(x_in.at[some], x_recv.at[q])
+        hvp_ref[some, :] = hvp_ref[some, :] + x_in[some, :].astype(f32)
+    for j in range(NZ - 1):
+        landed(z_in.at[j], z_recv.at[j])
+    out_ref[...] = (
+        own_half(0)[...].astype(f32) + z_in[0].astype(f32)
+        + z_in[1].astype(f32) + z_in[2].astype(f32)
+    ).astype(b16)
+    for copy in sent:
+        copy.wait_send()
+
+
+def fused(tokens, cotangent, expert_ids, combine, w_gate, w_up, w_down, tangent_gate):
+    count = lax.axis_size("expert")
+    n, top = expert_ids.shape
+    width, hidden = w_gate.shape[1:]
+    capacity = n * top * 9 // (8 * count)
+    total = count * capacity
+    b16, f32 = jnp.bfloat16, jnp.float32
+    dma = pltpu.SemaphoreType.DMA
+    pairs = NZ * NY
+    whole = pl.BlockSpec(memory_space=pltpu.VMEM)
+    hvp, out = pl.pallas_call(
+        functools.partial(kernel, capacity),
+        out_shape=(
+            jax.ShapeDtypeStruct((width // 2, hidden), f32),
+            jax.ShapeDtypeStruct((n, width), b16),
+        ),
+        in_specs=[whole] * 7,
+        out_specs=(whole, whole),
+        scratch_shapes=[
+            pltpu.VMEM((count, count, n), f32),
+            pltpu.VMEM((count * n, width), b16),
+            pltpu.VMEM((count * n, width), b16),
+            pltpu.VMEM((total, width), b16),
+            pltpu.VMEM((total, hidden), f32),
+            pltpu.VMEM((total, hidden), b16),
+            pltpu.VMEM((pairs, NC * n, width), b16),
+            pltpu.VMEM((pairs, n, width), b16),
+            pltpu.VMEM((NZ, n, width), b16),
+            pltpu.VMEM((NZ - 1, n, width), b16),
+            pltpu.VMEM((width // 2, hidden), b16),
+            pltpu.VMEM((width // 2, hidden), b16),
+            dma((3, 4 * NZ - 1)), dma((3, count)),
+            dma((pairs,)), dma((pairs,)),
+            dma((NZ,)), dma((NZ,)),
+            dma((NZ - 1,)), dma((NZ - 1,)),
+            dma((4,)), dma((4,)),
+        ],
+        compiler_params=pltpu.CompilerParams(
+            collective_id=0, has_side_effects=True, vmem_limit_bytes=63 * 1024 * 1024
+        ),
+    )(
+        weight_table(expert_ids, combine, count), tokens, cotangent,
+        w_gate[0], w_up[0], w_down[0], tangent_gate[0],
+    )
+    return hvp[None], out
+
+
+def per_device(*arrays):
+    if lax.axis_size("expert") == NZ * NY * NC and lax.axis_size("dp") == 2:
+        return fused(*arrays)
+    return gathered(*arrays)
+
+
 def solution(mesh):
     rows = P(("dp", "expert"), None)
     owned = P("expert", None, None)

time: 353 us -> 194 us (0.55)
  waiting for transfers between devices: 276 us -> 0 us
  Pallas kernels: 0 us -> 185 us
  matrix products: 50.1 us -> 0 us
  between operations: 13.8 us -> 0.65 us
  blocking collectives: 10.2 us -> 0 us
  local copies, waits for them, and re-layouts: 0.11 us -> 3.93 us
    pallas_call x0 -> x1, Pallas kernels: none -> 185 us  [fused(): pl.pallas_call(functools.partial(kernel, capacity), out_shape=(jax.ShapeD...]
    reduce_scatter x2 -> x0, waiting for transfers between devices: 151 us -> none  [the longest x1 110 us: per_device(): lax.psum_scatter(partial, 'expert', scatter_dimension=0, tiled=True)]
    all_gather x2 -> x0, waiting for transfers between devices: 123 us -> none  [the longest x1 64.9 us: per_device(): tokens_all = lax.all_gather(tokens, 'expert', axis=0)]
    dot_general x8 -> x0, matrix products: 50.1 us -> none  [the longest x1 14.2 us: per_device(): lax.dot_general(rows_flat, coeff, (((0,), (0,)), ((), ())), preferred_ele...]
    all_to_all x1 -> x0, blocking collectives: 10.2 us -> none  [per_device(): lax.all_to_all(table, 'expert', split_axis=0, concat_axis=0, tiled=True)]
    unnamed x10 -> x4, local copies, waits for them, and re-layouts: 0.03 us -> 3.93 us
  transfers between devices with their start and end apart: 4 -> 0, of which waited for: 4 -> 0; matrix products, arithmetic and copies ran while one was open for 9% -> 0% of each run, Pallas kernels for 0% -> 0%
where the time goes in v2:
time: 194 us; the launch traced here: 191 us
  Pallas kernels  185 us (95%)
  local copies, waits for them, and re-layouts  3.93 us (2%)
    pallas_call x1, Pallas kernels, fused(): pl.pallas_call(functools.partial(kernel, capacity), out_shape=(jax.ShapeD...  185 us
    unnamed x4, local copies, waits for them, and re-layouts  3.93 us

profile of v2, /device:TPU:13, one launch (start us, length us, event | category | flops | bytes accessed | tf_op | source)
XLA Modules:
  0.0 191.4 jit_solution(17840464888910863049)
XLA Ops:
  0.6 1.3 select_reduce_fusion
  1.9 185.5 %shard_map.95 = (f32[1024,512]{1,0:T(8,128)}, bf16[128,2048]{1,0:T(8,128)(2,1)}) custom-call(f32[16,128]{1,0:T(8,128)} %bitcast.11, bf16[128,2048]{1,0:T(8,128)(2,1)} %tokens_ref.1, bf16[128,2048]{1,0:T(8,128)(2,1)} %cot_ref.1, bf16[2048,512]{1,0:T(8,128)(2,1)} %bitcast.7, bf16[2048,512]{1,0:T(8,128)(2,1)} %bitcast.8, bf16[512,2048]{1,0:T(8,128)(2,1)} %bitcast.9, ...), custom_call_target="tpu_custom_call" | custom-call | tf_op jit(solution)/shard_map/pallas_call | solution.py:302
  187.4 0.0 copy-start
  187.4 3.1 %copy.14 = f32[1,1024,512]{2,1,0:T(8,128)} copy(f32[1,1024,512]{2,1,0:T(8,128)} %bitcast.6) | data formatting | bytes 4194304
  190.6 0.0 copy-done
  190.6 0.8 copy.15
Async XLA Ops:
  187.4 3.1 %copy-start = (bf16[128,2048]{1,0:T(8,128)(2,1)S(1)}, bf16[128,2048]{1,0:T(8,128)(2,1)}, u32[]{:S(2)}) copy-start(bf16[128,2048]{1,0:T(8,128)(2,1)} %get-tuple-element.9) | copy-start | bytes 1572868

commit v3 on v2

--- a/solution.py
+++ b/solution.py
@@ -109,7 +109,14 @@
 
     def begin(copy):
         copy.start()
-        sent.append(copy)
+        sent.append((None, lambda: copy))
+
+    def begin_if(test, make):
+        @pl.when(test)
+        def _():
+            make().start()
+
+        sent.append((test, make))
 
     fulls = (table, tok, cot)
     owns = (table_ref, tokens_ref, cot_ref)
@@ -123,22 +130,42 @@
     def arrived(a, b):
         remote(piece(a, b), piece(a, b), g_send.at[a, 0], g_recv.at[a, b], (dp, sibling)).wait_recv()
 
+    def block_copy(a, src, b, slot, peer):
+        return lambda: remote(src(), piece(a, b), g_send.at[a, slot], g_recv.at[a, b], peer)
+
     def send_own(a):
         send_block(a, owns[a], me, 0, (dp, across))
-        for j in range(1, NZ):
-            send_block(a, owns[a], me, j, (dp, at(zj(j), y, c)))
-        send_block(a, owns[a], me, NZ, (dp, sibling))
-
-    def pass_row(a, j):
-        b = at(zj(j), y, c)
-        arrived(a, b)
-        send_block(a, piece(a, b), b, NZ + j, (dp, across))
-        send_block(a, piece(a, b), b, 2 * NZ - 1 + j, (dp, sibling))
+        for slot, step in ((2, -1), (3, 1)):
+            near = z + step
+            begin_if(
+                (near >= 0) & (near < NZ),
+                block_copy(a, lambda: owns[a], me, slot, (dp, at(near, y, c))),
+            )
+        send_block(a, owns[a], me, 1, (dp, sibling))
+
+    def pass_row(a, d):
+        for side, step in enumerate((-1, 1)):
+            origin, onward = z + step * d, z - step
+            b = at(origin, y, c)
+            there = (origin >= 0) & (origin < NZ)
+
+            @pl.when(there)
+            def _():
+                arrived(a, b)
+
+            slot = 4 + (side * (NZ - 1) + d - 1) * 3
+            source = lambda a=a, b=b: piece(a, b)
+            begin_if(
+                there & (onward >= 0) & (onward < NZ),
+                block_copy(a, source, b, slot, (dp, at(onward, y, c))),
+            )
+            begin_if(there, block_copy(a, source, b, slot + 1, (dp, across)))
+            begin_if(there, block_copy(a, source, b, slot + 2, (dp, sibling)))
 
     def pass_across(a, j):
         b = at(zj(j), 1 - y, c)
         arrived(a, b)
-        send_block(a, piece(a, b), b, 3 * NZ - 1 + j, (dp, sibling))
+        send_block(a, piece(a, b), b, 6 * NZ - 2 + j, (dp, sibling))
 
     send_own(0)
     send_own(1)
@@ -216,12 +243,13 @@
         to_sibling(j0 + 1)
 
     group(0)
+    pass_row(2, 1)
     group(2)
+    pass_row(2, 2)
     for j in range(NZ):
         pass_across(0, j)
         pass_across(1, j)
-    for j in range(1, NZ):
-        pass_row(2, j)
+    pass_row(2, 3)
     group(4)
     group(6)
 
@@ -285,8 +313,13 @@
         own_half(0)[...].astype(f32) + z_in[0].astype(f32)
         + z_in[1].astype(f32) + z_in[2].astype(f32)
     ).astype(b16)
-    for copy in sent:
-        copy.wait_send()
+    for test, make in sent:
+        if test is None:
+            make().wait_send()
+        else:
+            @pl.when(test)
+            def _():
+                make().wait_send()
 
 
 def fused(tokens, cotangent, expert_ids, combine, w_gate, w_up, w_down, tangent_gate):
@@ -320,7 +353,7 @@
             pltpu.VMEM((NZ - 1, n, width), b16),
             pltpu.VMEM((width // 2, hidden), b16),
             pltpu.VMEM((width // 2, hidden), b16),
-            dma((3, 4 * NZ - 1)), dma((3, count)),
+            dma((3, 7 * NZ - 2)), dma((3, count)),
             dma((pairs,)), dma((pairs,)),
             dma((NZ,)), dma((NZ,)),
             dma((NZ - 1,)), dma((NZ - 1,)),

time: 194 us -> 171 us (0.88)
  Pallas kernels: 185 us -> 163 us
    pallas_call x1, Pallas kernels: 185 us -> 163 us  [fused(): pl.pallas_call(functools.partial(kernel, capacity), out_shape=(jax.ShapeD...]
where the time goes in v3:
time: 171 us; the launch traced here: 169 us
  Pallas kernels  163 us (95%)
  local copies, waits for them, and re-layouts  3.93 us (2%)
    pallas_call x1, Pallas kernels, fused(): pl.pallas_call(functools.partial(kernel, capacity), out_shape=(jax.ShapeD...  163 us
    unnamed x4, local copies, waits for them, and re-layouts  3.93 us

profile of v3, /device:TPU:13, one launch (start us, length us, event | category | flops | bytes accessed | tf_op | source)
XLA Modules:
  0.0 169.2 jit_solution(17296441467580968439)
XLA Ops:
  0.6 1.3 select_reduce_fusion
  1.9 163.3 %shard_map.95 = (f32[1024,512]{1,0:T(8,128)}, bf16[128,2048]{1,0:T(8,128)(2,1)}) custom-call(f32[16,128]{1,0:T(8,128)} %bitcast.11, bf16[128,2048]{1,0:T(8,128)(2,1)} %tokens_ref.1, bf16[128,2048]{1,0:T(8,128)(2,1)} %cot_ref.1, bf16[2048,512]{1,0:T(8,128)(2,1)} %bitcast.7, bf16[2048,512]{1,0:T(8,128)(2,1)} %bitcast.8, bf16[512,2048]{1,0:T(8,128)(2,1)} %bitcast.9, ...), custom_call_target="tpu_custom_call" | custom-call | tf_op jit(solution)/shard_map/pallas_call | solution.py:335
  165.3 0.0 copy-start
  165.3 3.1 %copy.14 = f32[1,1024,512]{2,1,0:T(8,128)} copy(f32[1,1024,512]{2,1,0:T(8,128)} %bitcast.6) | data formatting | bytes 4194304
  168.4 0.0 copy-done
  168.4 0.8 copy.15
Async XLA Ops:
  165.3 3.1 %copy-start = (bf16[128,2048]{1,0:T(8,128)(2,1)S(1)}, bf16[128,2048]{1,0:T(8,128)(2,1)}, u32[]{:S(2)}) copy-start(bf16[128,2048]{1,0:T(8,128)(2,1)} %get-tuple-element.9) | copy-start | bytes 1572868
